TPU v7x, 32 devices: a whole 2x2x4 slice. The times are simulated.
32 devices in a mesh: day: 4 (over y, x), lon: 4 (over z), lat: 2 (over core).
Axes of the slice: x: 2, y: 2, z: 4, core: 2. Of those that a mesh axis runs over, the one named last changes fastest.
Arguments:
- historical_runs: bfloat16 [64, 5, 3, 180, 256], P('day', None, None, 'lon', 'lat'), may hold values from -6 to 6
- todays_outlook: bfloat16 [5, 3, 180, 256], P(None, None, 'lon', 'lat'), may hold values from -6 to 6
- variable_importance: float32 [5], replicated, may hold values from 0.3 to 3
- verifying_measurements: bfloat16 [64, 3, 180, 256], P('day', None, 'lon', 'lat'), may hold values from -6 to 6
- matching_dates_chosen: int32 [3, 180, 256, 20], P(None, 'lon', ('lat', 'day')), may hold values from 0 to 63, all different within a row
Outputs:
- metric: float32 [64, 3, 180, 256], P('day', None, 'lon', 'lat')
- prediction: float32 [3, 180, 256], P(None, 'lon', ('lat', 'day'))
Inputs may be any that keep to these rules, and one draw needn't show every extreme that they name: `matching_dates_chosen`: each cell and lead names 20 different days.
All inputs are finite; a program needn't handle non-finite values.
Results may differ from a plain program's by a relative error of at most 0.0028.
Values may be sent and summed in bfloat16 or wider, within the bound.
A program may use at most 64 MiB of HBM per device.

v0:
```python
import jax
import jax.numpy as jnp
from jax import lax
from jax.sharding import PartitionSpec as P


def extended(block, sides, width, periodic):
    for axis, dim in sides:
        count = lax.axis_size(axis)
        forward = [(i, i + 1) for i in range(count - 1)]
        if periodic:
            forward.append((count - 1, 0))
        backward = [(target, source) for source, target in forward]
        low = lax.ppermute(
            lax.slice_in_dim(block, block.shape[dim] - width, None, axis=dim), axis, forward
        )
        high = lax.ppermute(lax.slice_in_dim(block, 0, width, axis=dim), axis, backward)
        block = jnp.concatenate([low, block, high], axis=dim)
    return block


def window_sum(values, reduce_axis, count):
    total = lax.slice_in_dim(values, 0, count, axis=reduce_axis)
    for shift in range(1, 7):
        total = total + lax.slice_in_dim(values, shift, shift + count, axis=reduce_axis)
    return total


def band_sum(rimmed, count):
    rows_in = lax.broadcasted_iota(jnp.int32, (count + 6, count), 0)
    cols_out = lax.broadcasted_iota(jnp.int32, (count + 6, count), 1)
    offset = rows_in - cols_out
    band = ((offset >= 0) & (offset <= 6)).astype(jnp.float32)
    return jnp.einsum("dlxi,ij->dlxj", rimmed, band, precision=lax.Precision.HIGHEST)


def lead_box(boxed):
    padded = jnp.pad(boxed, ((0, 0), (1, 1), (0, 0), (0, 0)))
    return (padded[:, :-2] + padded[:, 1:-1] + padded[:, 2:]) / 147.0


def selection(chosen, count):
    days_col = jnp.arange(count, dtype=jnp.int32)[:, None, None, None]
    picked = jnp.zeros((count,) + chosen.shape[:-1], jnp.float32)
    for slot in range(chosen.shape[-1]):
        picked = picked + (chosen[None, :, :, :, slot] == days_col).astype(jnp.float32)
    return picked


def on_device(
    historical_runs,
    todays_outlook,
    variable_importance,
    verifying_measurements,
    matching_dates_chosen,
):
    count_x = historical_runs.shape[3]
    count_y = historical_runs.shape[4]
    scale = variable_importance[None, :, None, None, None]
    layered_grids = jnp.concatenate([todays_outlook[None], historical_runs], axis=0)
    wider = extended(layered_grids, (("lon", 3),), 3, True)
    wider = extended(wider, (("lat", 4),), 3, False)
    diff = wider[1:].astype(jnp.float32) - wider[0:1].astype(jnp.float32)
    squares = jnp.sum(scale * diff * diff, axis=1)
    boxed = band_sum(window_sum(squares, 2, count_x), count_y)
    metric = lead_box(boxed)
    weights = (1.0 / (metric + 1e-05)).astype(jnp.bfloat16)
    got_weights, got_obs = (
        lax.all_to_all(weights, "day", split_axis=3, concat_axis=0, tiled=True),
        lax.all_to_all(verifying_measurements, "day", split_axis=3, concat_axis=0, tiled=True),
    )
    picked = selection(matching_dates_chosen, got_weights.shape[0])
    weight_f = got_weights.astype(jnp.float32) * picked
    numerator = jnp.sum(weight_f * got_obs.astype(jnp.float32), axis=0)
    denominator = jnp.sum(weight_f, axis=0)
    return (metric, numerator / denominator)


def solution(mesh):
    in_specs = (
        P("day", None, None, "lon", "lat"),
        P(None, None, "lon", "lat"),
        P(),
        P("day", None, "lon", "lat"),
        P(None, "lon", ("lat", "day"), None),
    )
    out_specs = (P("day", None, "lon", "lat"), P(None, "lon", ("lat", "day")))
    return jax.shard_map(
        on_device, mesh=mesh, in_specs=in_specs, out_specs=out_specs, check_vma=False
    )
```

profile of v0, /device:TPU:0, one launch (start us, length us, event | category | flops | bytes accessed | tf_op | source)
XLA Modules:
  0.0 145.0 jit_solution(17185997717775241408)
XLA Ops:
  0.6 2.6 %copy.115 = bf16[16,5,3,45,128]{4,3,2,1,0:T(8,128)(2,1)S(1)} copy(bf16[16,5,3,45,128]{4,0,3,2,1:T(8,128)(2,1)} %param.5) | data formatting | bytes 5529600 | tf_op args[0]
  3.5 3.1 %collective-permute-start = (bf16[17,5,3,3,128]{4,3,2,1,0:T(4,128)(2,1)S(1)}, bf16[17,5,3,3,128]{4,3,2,1,0:T(4,128)(2,1)S(1)}, u32[]{:S(2)}, u32[]{:S(2)}) collective-permute-start(bf16[17,5,3,3,128]{4,3,2,1,0:T(4,128)(2,1)S(1)} %get-tuple-element.18), channel_id=1, source_target_pairs={{0,2},{2,4},{4,6},{6,0},{1,3},{3,5},{5,7},{7,1},{8,10},{10,12},{12... | collective-permute-start | bytes 587528 | tf_op jit(solution)/shard_map/ppermute | solution.py:14
  6.6 2.1 %collective-permute-start.1 = (bf16[17,5,3,3,128]{4,3,2,1,0:T(4,128)(2,1)S(1)}, bf16[17,5,3,3,128]{4,3,2,1,0:T(4,128)(2,1)S(1)}, u32[]{:S(2)}, u32[]{:S(2)}) collective-permute-start(bf16[17,5,3,3,128]{4,3,2,1,0:T(4,128)(2,1)S(1)} %get-tuple-element.19), channel_id=1, source_target_pairs={{2,0},{4,2},{6,4},{0,6},{3,1},{5,3},{7,5},{1,7},{10,8},{12,10},{14... | collective-permute-start | bytes 587528 | tf_op jit(solution)/shard_map/ppermute | solution.py:17
  8.7 7.1 %collective-permute-done = bf16[17,5,3,3,128]{4,3,2,1,0:T(4,128)(2,1)S(1)} collective-permute-done((bf16[17,5,3,3,128]{4,3,2,1,0:T(4,128)(2,1)S(1)}, bf16[17,5,3,3,128]{4,3,2,1,0:T(4,128)(2,1)S(1)}, u32[]{:S(2)}, u32[]{:S(2)}) %collective-permute-start) | collective-permute-done | bytes 195872 | tf_op jit(solution)/shard_map/ppermute | solution.py:14
  15.7 4.2 %collective-permute-done.1 = bf16[17,5,3,3,128]{4,3,2,1,0:T(4,128)(2,1)S(1)} collective-permute-done((bf16[17,5,3,3,128]{4,3,2,1,0:T(4,128)(2,1)S(1)}, bf16[17,5,3,3,128]{4,3,2,1,0:T(4,128)(2,1)S(1)}, u32[]{:S(2)}, u32[]{:S(2)}) %collective-permute-start.1) | collective-permute-done | bytes 195872 | tf_op jit(solution)/shard_map/ppermute | solution.py:17
  19.9 2.2 %pad_maximum_fusion.1 = bf16[17,5,3,51,128]{4,3,2,1,0:T(8,128)(2,1)S(1)} fusion(bf16[17,5,3,3,128]{4,3,2,1,0:T(4,128)(2,1)S(1)} %collective-permute-done.1, bf16[16,5,3,45,128]{4,3,2,1,0:T(8,128)(2,1)S(1)} %copy.115, bf16[1,5,3,45,128]{4,3,2,1,0:T(8,128)(2,1)S(1)} %bitcast.74, bf16[17,5,3,3,128]{4,3,2,1,0:T(4,128)(2,1)S(1)} %collective-permute-done), kind=kLoop, calls=%fused_computation.6 | loop fusion | flops 13317120 | bytes 6658560 | tf_op jit(solution)/shard_map/concatenate | solution.py:18
  22.1 4.5 %fusion.20 = (bf16[17,5,3,51,3]{4,3,2,1,0:T(8,128)(2,1)}, bf16[17,5,3,51,3]{4,3,2,1,0:T(8,128)(2,1)}) fusion(bf16[17,5,3,51,128]{4,3,2,1,0:T(8,128)(2,1)S(1)} %pad_maximum_fusion.1), kind=kLoop, calls=%fused_computation.56 | loop fusion | bytes 312120 | tf_op jit(solution)/shard_map/slice | solution.py:15
  26.6 4.5 %copy.116 = bf16[17,5,3,51,3]{3,4,2,1,0:T(4,128)(2,1)} copy(bf16[17,5,3,51,3]{4,3,2,1,0:T(8,128)(2,1)} %get-tuple-element.16) | data formatting | bytes 156060 | tf_op jit(solution)/shard_map/slice | solution.py:15
  31.1 2.0 %collective-permute-start.2 = (bf16[17,5,3,51,3]{3,4,2,1,0:T(4,128)(2,1)}, bf16[17,5,3,51,3]{3,4,2,1,0:T(4,128)(2,1)}, u32[]{:S(2)}, u32[]{:S(2)}) collective-permute-start(bf16[17,5,3,51,3]{3,4,2,1,0:T(4,128)(2,1)} %copy.116), channel_id=1, source_target_pairs={{0,1},{2,3},{4,5},{6,7},{8,9},{10,11},{12,13},{14,15},{16,17},{18,... | collective-permute-start | bytes 234098 | tf_op jit(solution)/shard_map/ppermute | solution.py:14
  33.1 4.5 %copy.117 = bf16[17,5,3,51,3]{3,4,2,1,0:T(4,128)(2,1)} copy(bf16[17,5,3,51,3]{4,3,2,1,0:T(8,128)(2,1)} %get-tuple-element.17) | data formatting | bytes 156060 | tf_op jit(solution)/shard_map/slice | solution.py:17
  37.5 1.3 collective-permute-start.3
  38.8 2.8 %copy.142 = bf16[16,3,45,128]{2,0,1,3:T(8,128)(2,1)} copy(bf16[16,3,45,128]{3,0,2,1:T(8,128)(2,1)} %param.8) | data formatting | bytes 1105920 | tf_op args[3]
  41.6 4.5 %reshape.75 = bf16[4,2,34560]{2,1,0:T(2,128)(2,1)} reshape(bf16[128,3,16,45]{3,2,1,0:T(8,128)(2,1)} %bitcast.72) | data formatting | bytes 1105920
  46.1 4.3 %all-to-all-start.1 = ((bf16[4,2,34560]{2,1,0:T(2,128)(2,1)}), bf16[4,2,34560]{2,1,0:T(2,128)(2,1)}, u32[]{:S(2)}, u32[]{:S(2)}) async-start(bf16[4,2,34560]{2,1,0:T(2,128)(2,1)} %reshape.75), calls=%async_computation.1 | async-start | bytes 1105920 | tf_op jit(solution)/shard_map/all_to_all | solution.py:70
  50.5 4.3 %copy.118 = bf16[17,5,3,51,3]{4,3,2,1,0:T(8,128)(2,1)} copy(bf16[17,5,3,51,3]{3,4,2,1,0:T(4,128)(2,1)} %collective-permute-done.2) | data formatting | bytes 156060 | tf_op jit(solution)/shard_map/ppermute | solution.py:14
  54.8 4.5 %copy.119 = bf16[17,5,3,51,3]{4,3,2,1,0:T(8,128)(2,1)} copy(bf16[17,5,3,51,3]{3,4,2,1,0:T(4,128)(2,1)} %collective-permute-done.3) | data formatting | bytes 156060 | tf_op jit(solution)/shard_map/ppermute | solution.py:17
  59.3 1.6 %fusion.7 = f32[5,3,51,134]{3,2,1,0:T(8,128)S(1)} fusion(bf16[17,5,3,51,3]{4,3,2,1,0:T(8,128)(2,1)} %copy.119, bf16[17,5,3,51,3]{4,3,2,1,0:T(8,128)(2,1)} %copy.118, bf16[17,5,3,3,128]{4,3,2,1,0:T(4,128)(2,1)} %copy-done.3, bf16[17,5,3,3,128]{4,3,2,1,0:T(4,128)(2,1)S(1)} %collective-permute-done, bf16[16,5,3,45,128]{4,3,2,1,0:T(8,128)(2,1)S(1)} %copy.115, ...), kind=kLoop, calls=%fused_computation.22 | loop fusion | flops 1332630 | bytes 3895380 | tf_op jit(solution)/shard_map/sub | solution.py:63
  62.7 7.8 %pad_maximum_fusion = bf16[17,5,3,51,134]{4,3,2,1,0:T(8,128)(2,1)S(1)} fusion(bf16[17,5,3,51,3]{4,3,2,1,0:T(8,128)(2,1)S(1)} %copy-done.1, bf16[17,5,3,3,128]{4,3,2,1,0:T(4,128)(2,1)S(1)} %copy-done.4, bf16[16,5,3,45,128]{4,3,2,1,0:T(8,128)(2,1)S(1)} %copy.115, bf16[1,5,3,45,128]{4,3,2,1,0:T(8,128)(2,1)S(1)} %bitcast.76, ...), kind=kLoop, calls=%fused_computation.2 | loop fusion | flops 20912040 | bytes 6970680 | tf_op jit(solution)/shard_map/concatenate | solution.py:18
  70.5 2.6 %fusion = f32[16,3,51,134]{3,2,1,0:T(8,128)S(1)} fusion(bf16[17,5,3,51,134]{4,3,2,1,0:T(8,128)(2,1)S(1)} %pad_maximum_fusion, f32[5,3,51,134]{3,2,1,0:T(8,128)S(1)} %fusion.7, f32[5]{0:T(128)S(1)} %copy-done.13), kind=kLoop, calls=%fused_computation.1 | loop fusion | flops 7872768 | bytes 5002508 | tf_op jit(solution)/shard_map/reduce_sum | solution.py:64
  73.1 2.6 %fusion.2 = f32[16,3,45,128]{3,2,1,0:T(8,128)S(1)} fusion(f32[16,3,51,134]{3,2,1,0:T(8,128)S(1)} %fusion), kind=kOutput, calls=%fused_computation.8 | convolution fusion | flops 446385088 | bytes 17620992 | tf_op jit(solution)/shard_map/dlxi,ij->dlxj/dot_general | solution.py:34
  75.9 1.1 copy.120
  77.0 3.5 %reshape.73 = bf16[4,2,34560]{2,1,0:T(2,128)(2,1)} reshape(bf16[128,3,16,45]{3,2,1,0:T(8,128)(2,1)S(1)} %bitcast.69) | data formatting | bytes 1105920
  80.6 4.0 %all-to-all-start = ((bf16[4,2,34560]{2,1,0:T(2,128)(2,1)}), bf16[4,2,34560]{2,1,0:T(2,128)(2,1)S(1)}, u32[]{:S(2)}, u32[]{:S(2)}) async-start(bf16[4,2,34560]{2,1,0:T(2,128)(2,1)} %reshape.73), calls=%async_computation | async-start | bytes 1105920 | tf_op jit(solution)/shard_map/all_to_all | solution.py:69
  84.5 1.3 slice_bitcast_fusion.19
  99.3 1.3 copy.144
  100.6 5.2 %reshape.76 = bf16[128,3,16,45]{3,2,1,0:T(8,128)(2,1)S(1)} reshape(bf16[4,2,34560]{2,1,0:T(2,128)(2,1)} %all-to-all-done.1) | data formatting | bytes 1105920
  105.8 1.3 copy.143
  107.1 3.3 %reshape.71 = f32[16,3,45,4,32]{4,3,0,2,1:T(4,128)} reshape(bf16[16,3,45,128]{3,0,2,1:T(8,128)(2,1)S(1)} %copy.143) | data formatting | bytes 1658880 | tf_op jit(solution)/shard_map/convert_element_type | solution.py:74
  110.4 4.4 %reshape.74 = bf16[128,3,16,45]{3,2,1,0:T(8,128)(2,1)S(1)} reshape(bf16[4,2,34560]{2,1,0:T(2,128)(2,1)S(1)} %all-to-all-done) | data formatting | bytes 1105920
  114.9 1.3 copy.121
  116.2 3.3 %reshape.70 = f32[16,3,45,4,32]{4,3,0,2,1:T(4,128)} reshape(bf16[16,3,45,128]{3,0,2,1:T(8,128)(2,1)S(1)} %copy.121) | data formatting | bytes 1658880 | tf_op jit(solution)/shard_map/convert_element_type | solution.py:73
  119.6 24.6 %fusion.18 = (f32[3,45,32]{2,1,0:T(8,128)S(1)}, f32[3,45,32]{2,1,0:T(8,128)S(1)}) fusion(f32[16,3,45,4,32]{4,3,0,2,1:T(4,128)} %reshape.71, s32[3,45,32]{2,1,0:T(8,128)} %copy.141, s32[3,45,32]{2,1,0:T(8,128)} %copy.140, s32[3,45,32]{2,1,0:T(8,128)} %copy.139, s32[3,45,32]{2,1,0:T(8,128)} %copy.138, s32[3,45,32]{2,1,0:T(8,128)} %copy.137, ...), kind=kLoop, calls=%fused_computation.55 | loop fusion | flops 17409600 | bytes 2592256 | tf_op jit(solution)/shard_map/reduce_sum | solution.py:75
  (58 shorter events, 16.6 us)
Async XLA Ops:
  0.6 2.6 %copy-start.2 = (bf16[5,3,45,128]{3,2,1,0:T(8,128)(2,1)S(1)}, bf16[5,3,45,128]{3,2,1,0:T(8,128)(2,1)}, u32[]{:S(2)}) copy-start(bf16[5,3,45,128]{3,2,1,0:T(8,128)(2,1)} %param.6) | copy-start | bytes 518404
  3.5 12.3 %collective-permute-start = (bf16[17,5,3,3,128]{4,3,2,1,0:T(4,128)(2,1)S(1)}, bf16[17,5,3,3,128]{4,3,2,1,0:T(4,128)(2,1)S(1)}, u32[]{:S(2)}, u32[]{:S(2)}) collective-permute-start(bf16[17,5,3,3,128]{4,3,2,1,0:T(4,128)(2,1)S(1)} %get-tuple-element.18), channel_id=1, source_target_pairs={{0,2},{2,4},{4,6},{6,0},{1,3},{3,5},{5,7},{7,1},{8,10},{10,12},{12... | collective-permute-start | bytes 587528 | tf_op jit(solution)/shard_map/ppermute | solution.py:14
  6.6 13.3 %collective-permute-start.1 = (bf16[17,5,3,3,128]{4,3,2,1,0:T(4,128)(2,1)S(1)}, bf16[17,5,3,3,128]{4,3,2,1,0:T(4,128)(2,1)S(1)}, u32[]{:S(2)}, u32[]{:S(2)}) collective-permute-start(bf16[17,5,3,3,128]{4,3,2,1,0:T(4,128)(2,1)S(1)} %get-tuple-element.19), channel_id=1, source_target_pairs={{2,0},{4,2},{6,4},{0,6},{3,1},{5,3},{7,5},{1,7},{10,8},{12,10},{14... | collective-permute-start | bytes 587528 | tf_op jit(solution)/shard_map/ppermute | solution.py:17
  19.9 6.7 %copy-start.3 = (bf16[17,5,3,3,128]{4,3,2,1,0:T(4,128)(2,1)}, bf16[17,5,3,3,128]{4,3,2,1,0:T(4,128)(2,1)S(1)}, u32[]{:S(2)}) copy-start(bf16[17,5,3,3,128]{4,3,2,1,0:T(4,128)(2,1)S(1)} %collective-permute-done.1) | copy-start | bytes 587524
  31.1 19.4 %collective-permute-start.2 = (bf16[17,5,3,51,3]{3,4,2,1,0:T(4,128)(2,1)}, bf16[17,5,3,51,3]{3,4,2,1,0:T(4,128)(2,1)}, u32[]{:S(2)}, u32[]{:S(2)}) collective-permute-start(bf16[17,5,3,51,3]{3,4,2,1,0:T(4,128)(2,1)} %copy.116), channel_id=1, source_target_pairs={{0,1},{2,3},{4,5},{6,7},{8,9},{10,11},{12,13},{14,15},{16,17},{18,... | collective-permute-start | bytes 234098 | tf_op jit(solution)/shard_map/ppermute | solution.py:14
  37.5 17.3 %collective-permute-start.3 = (bf16[17,5,3,51,3]{3,4,2,1,0:T(4,128)(2,1)}, bf16[17,5,3,51,3]{3,4,2,1,0:T(4,128)(2,1)}, u32[]{:S(2)}, u32[]{:S(2)}) collective-permute-start(bf16[17,5,3,51,3]{3,4,2,1,0:T(4,128)(2,1)} %copy.117), channel_id=1, source_target_pairs={{1,0},{3,2},{5,4},{7,6},{9,8},{11,10},{13,12},{15,14},{17,16},{19,... | collective-permute-start | bytes 234098 | tf_op jit(solution)/shard_map/ppermute | solution.py:17
  46.1 34.4 %all-to-all-start.1 = ((bf16[4,2,34560]{2,1,0:T(2,128)(2,1)}), bf16[4,2,34560]{2,1,0:T(2,128)(2,1)}, u32[]{:S(2)}, u32[]{:S(2)}) async-start(bf16[4,2,34560]{2,1,0:T(2,128)(2,1)} %reshape.75), calls=%async_computation.1 | async-start | bytes 1105920 | tf_op jit(solution)/shard_map/all_to_all | solution.py:70
  59.3 2.3 %copy-start = (bf16[17,5,3,51,3]{4,3,2,1,0:T(8,128)(2,1)S(1)}, bf16[17,5,3,51,3]{4,3,2,1,0:T(8,128)(2,1)}, u32[]{:S(2)}) copy-start(bf16[17,5,3,51,3]{4,3,2,1,0:T(8,128)(2,1)} %copy.118) | copy-start | bytes 234094
  59.3 3.4 %copy-start.1 = (bf16[17,5,3,51,3]{4,3,2,1,0:T(8,128)(2,1)S(1)}, bf16[17,5,3,51,3]{4,3,2,1,0:T(8,128)(2,1)}, u32[]{:S(2)}) copy-start(bf16[17,5,3,51,3]{4,3,2,1,0:T(8,128)(2,1)} %copy.119) | copy-start | bytes 234094
  59.3 3.4 %copy-start.4 = (bf16[17,5,3,3,128]{4,3,2,1,0:T(4,128)(2,1)S(1)}, bf16[17,5,3,3,128]{4,3,2,1,0:T(4,128)(2,1)}, u32[]{:S(2)}) copy-start(bf16[17,5,3,3,128]{4,3,2,1,0:T(4,128)(2,1)} %copy-done.3) | copy-start | bytes 587524
  62.7 7.8 %copy-start.13 = (f32[5]{0:T(128)S(1)}, f32[5]{0:T(128)}, u32[]{:S(2)}) copy-start(f32[5]{0:T(128)} %param.7) | copy-start | bytes 64
  80.6 29.9 %all-to-all-start = ((bf16[4,2,34560]{2,1,0:T(2,128)(2,1)}), bf16[4,2,34560]{2,1,0:T(2,128)(2,1)S(1)}, u32[]{:S(2)}, u32[]{:S(2)}) async-start(bf16[4,2,34560]{2,1,0:T(2,128)(2,1)} %reshape.73), calls=%async_computation | async-start | bytes 1105920 | tf_op jit(solution)/shard_map/all_to_all | solution.py:69
  110.4 9.2 %copy-start.5 = (s32[3,45,32]{2,1,0:T(8,128)S(1)}, s32[3,45,32]{2,1,0:T(8,128)}, u32[]{:S(2)}) copy-start(s32[3,45,32]{2,1,0:T(8,128)} %copy.125) | copy-start | bytes 51844
  110.4 9.2 %copy-start.6 = (s32[3,45,32]{2,1,0:T(8,128)S(1)}, s32[3,45,32]{2,1,0:T(8,128)}, u32[]{:S(2)}) copy-start(s32[3,45,32]{2,1,0:T(8,128)} %copy.126) | copy-start | bytes 51844
  110.4 9.2 %copy-start.7 = (s32[3,45,32]{2,1,0:T(8,128)S(1)}, s32[3,45,32]{2,1,0:T(8,128)}, u32[]{:S(2)}) copy-start(s32[3,45,32]{2,1,0:T(8,128)} %copy.127) | copy-start | bytes 51844
  110.4 9.2 %copy-start.8 = (s32[3,45,32]{2,1,0:T(8,128)S(1)}, s32[3,45,32]{2,1,0:T(8,128)}, u32[]{:S(2)}) copy-start(s32[3,45,32]{2,1,0:T(8,128)} %copy.128) | copy-start | bytes 51844
  110.4 9.2 %copy-start.9 = (s32[3,45,32]{2,1,0:T(8,128)S(1)}, s32[3,45,32]{2,1,0:T(8,128)}, u32[]{:S(2)}) copy-start(s32[3,45,32]{2,1,0:T(8,128)} %copy.129) | copy-start | bytes 51844
  110.4 9.2 %copy-start.10 = (s32[3,45,32]{2,1,0:T(8,128)S(1)}, s32[3,45,32]{2,1,0:T(8,128)}, u32[]{:S(2)}) copy-start(s32[3,45,32]{2,1,0:T(8,128)} %copy.130) | copy-start | bytes 51844
  110.4 9.2 %copy-start.11 = (s32[3,45,32]{2,1,0:T(8,128)S(1)}, s32[3,45,32]{2,1,0:T(8,128)}, u32[]{:S(2)}) copy-start(s32[3,45,32]{2,1,0:T(8,128)} %copy.131) | copy-start | bytes 51844
  110.4 9.2 %copy-start.12 = (s32[3,45,32]{2,1,0:T(8,128)S(1)}, s32[3,45,32]{2,1,0:T(8,128)}, u32[]{:S(2)}) copy-start(s32[3,45,32]{2,1,0:T(8,128)} %copy.132) | copy-start | bytes 51844
where the time goes:
time: 147 us; the launch traced here: 145 us
  local copies, waits for them, and re-layouts  74.3 us (51%)
  other arithmetic  39.2 us (27%)
  starting transfers between devices  16.7 us (11%)
  waiting for transfers between devices  11.3 us (8%)
  matrix products  2.55 us (2%)
    unnamed x36, local copies, waits for them, and re-layouts  26.9 us
    reduce_sum x1, other arithmetic, on_device(): denominator = jnp.sum(weight_f, axis=0)  24.6 us
    eq x22, local copies, waits for them, and re-layouts, selection(): chosen[None, :, :, :, slot] == days_col  14.7 us
    concatenate x2, other arithmetic, extended(): block = jnp.concatenate([low, block, high], axis=dim)  9.97 us
    slice x2, local copies, waits for them, and re-layouts, extended(): lax.slice_in_dim(block, block.shape[dim] - width, None, axis=dim)  8.96 us
    ppermute x2, waiting for transfers between devices, extended(): lax.ppermute(lax.slice_in_dim(block, block.shape[dim] - width, None, axis...  7.09 us
    ppermute x2, starting transfers between devices, extended(): lax.ppermute(lax.slice_in_dim(block, block.shape[dim] - width, None, axis...  5.06 us
    slice x1, local copies, waits for them, and re-layouts, extended(): lax.slice_in_dim(block, 0, width, axis=dim)  4.48 us
  transfers between devices with their start and end apart: 6, of which 2 were waited for; matrix products, arithmetic and copies ran while one was open for 45% of the time, Pallas kernels for 0%

commit v1 on v0

v1 whole, which is shorter than its diff:
```python
import functools

import jax
import jax.numpy as jnp
from jax import lax
from jax.experimental import pallas as pl
from jax.experimental.pallas import tpu as pltpu
from jax.sharding import PartitionSpec as P

RIM = 3
SLOT = 8
F32 = jnp.float32
BF16 = jnp.bfloat16


def kernel(
    days, lons, runs, outlook, scale, obs, chosen, metric_out, prediction_out,
    outlook_f, lhs, band, boxed, edge, edge_in, corner, corner_in, rim, rim_in,
    bits, bits_t, packed, mask_send, mask_in, part, part_send, part_in, flip,
    near_send, near_recv, mask_ssem, mask_rsem, part_ssem, part_rsem,
):
    variables, leads, cols, own_days, rows = runs.shape
    matches = chosen.shape[1]
    share = rows // days
    groups = -(-cols // days)
    per_tile = rows // SLOT
    day, lon, lat = lax.axis_index("day"), lax.axis_index("lon"), lax.axis_index("lat")
    left, right = lax.rem(lon + lons - 1, lons), lax.rem(lon + 1, lons)
    other = 1 - lat

    nearby = [
        {"lon": left}, {"lon": right},
        {"lon": left, "lat": other}, {"lon": right, "lat": other},
        {"lat": other},
    ]
    owners = [lax.rem(day + step, days) for step in range(days)]
    barrier = pltpu.get_barrier_semaphore()
    for device in nearby + [{"day": owner} for owner in owners[1:]]:
        pl.semaphore_signal(barrier, inc=1, device_id=device, device_id_type=pl.DeviceIdType.MESH)

    lane = lax.broadcasted_iota(jnp.int32, (own_days, rows), 1)
    slot_of = lane // SLOT
    part_of = lane // share

    def send(src, dst, ssem, rsem, device):
        copy = pltpu.make_async_remote_copy(
            src_ref=src, dst_ref=dst, send_sem=ssem, recv_sem=rsem,
            device_id=device, device_id_type=pl.DeviceIdType.MESH,
        )
        copy.start()
        return copy

    for p in range(variables):
        for l in range(leads):
            outlook_f[p * leads + l] = outlook[p, l].astype(F32)

    def squares(l, x):
        total = jnp.zeros((own_days, rows), F32)
        for p in range(variables):
            diff = runs[p, l, x].astype(F32) - outlook_f[p * leads + l, pl.ds(x, 1), :]
            total = total + scale[p] * (diff * diff)
        return total.astype(BF16)

    def edge_columns(x, side):
        for l in range(leads):
            value = squares(l, x + side * (cols - RIM))
            lhs[l, x + side * (cols - RIM) + RIM, :, :rows] = value
            edge[side, l * RIM + x] = value

    for side in range(2):
        @pl.loop(0, RIM)
        def _(x):
            edge_columns(x, side)
        total = jnp.zeros((own_days, rows), F32)
        for s in range(leads * RIM):
            moved = pltpu.roll(edge[side, s].astype(F32), RIM + SLOT * s, 1)
            total = jnp.where(slot_of == s, moved, total)
        corner[side] = total.astype(BF16)

    pl.semaphore_wait(barrier, len(nearby) + days - 1)
    near = []
    for side, (device, across) in enumerate([(nearby[0], nearby[2]), (nearby[1], nearby[3])]):
        near.append(send(edge.at[side], edge_in.at[1 - side], near_send.at[side], near_recv.at[side], device))
        near.append(send(corner.at[side], corner_in.at[1 - side], near_send.at[2 + side], near_recv.at[2 + side], across))

    words = days * own_days // 32
    targets_per_word = 32 // own_days
    for t in range(bits.shape[0]):
        bits[t] = jnp.zeros((rows, rows), jnp.int32)
    for l in range(leads):
        sums = [jnp.zeros((share, cols), jnp.int32) for _ in range(words)]
        for k in range(matches):
            index = chosen[l, k]
            bit = lax.shift_left(jnp.ones_like(index), index & 31)
            word = lax.shift_right_logical(index, jnp.full_like(index, 5))
            for w in range(words):
                sums[w] = sums[w] | jnp.where(word == w, bit, 0)
        for w in range(words):
            c = w * leads + l
            at = (c % days) * share
            bits[c // days, at:at + share, :cols] = sums[w]
    for t in range(bits.shape[0]):
        bits_t[t] = bits[t].T
    group_lane = lax.broadcasted_iota(jnp.int32, (groups, rows), 1) // share
    for c in range(words * leads):
        total = jnp.zeros((groups, rows), jnp.int32)
        for i in range(days):
            moved = bits_t[c // days, pl.ds(i, groups, stride=days), :]
            shift = (share * (i - c % days)) % rows
            if shift:
                moved = pltpu.roll(moved, shift, 1)
            total = jnp.where(group_lane == i, moved, total)
        packed[c, :groups] = total

    day_row = lax.broadcasted_iota(jnp.int32, (own_days, rows), 0)

    def expand(owner, store):
        shift = day_row + lax.rem(owner, targets_per_word) * own_days
        base = (owner // targets_per_word) * leads
        for l in range(leads):
            @pl.loop(0, groups)
            def _(q):
                row = jnp.broadcast_to(packed[base + l, pl.ds(q, 1), :], (own_days, rows))
                store(l, q, (lax.shift_right_logical(row, shift) & 1).astype(F32).astype(BF16))

    masks = []
    for step in range(1, days):
        def store(l, q, value):
            mask_send[step - 1, l, q] = value
        expand(owners[step], store)
        masks.append(send(
            mask_send.at[step - 1], mask_in.at[day], mask_ssem.at[step - 1], mask_rsem.at[step - 1],
            {"day": owners[step]},
        ))

    @pl.loop(RIM, cols - RIM)
    def _(x):
        for l in range(leads):
            lhs[l, x + RIM, :, :rows] = squares(l, x)

    @pl.loop(0, leads)
    def _(l):
        for g in range(rim.shape[1]):
            total = jnp.zeros((own_days, rows), F32)
            for s in range(min(per_tile, cols - g * per_tile)):
                tile = lhs[l, g * per_tile + s + RIM, :, :rows].astype(F32)
                total = jnp.where(slot_of == s, pltpu.roll(tile, (RIM + SLOT * s) % rows, 1), total)
            rim[l, g] = total.astype(BF16)

    near.append(send(rim, rim_in, near_send.at[4], near_recv.at[4], nearby[4]))

    def own_store(l, q, value):
        mask_in[day, l, q] = value
    expand(owners[0], own_store)

    source = lax.broadcasted_iota(jnp.int32, (2 * rows, rows), 0)
    target = lax.broadcasted_iota(jnp.int32, (2 * rows, rows), 1)
    beyond = source - rows
    place = beyond - RIM + rows * other
    first = RIM * other
    inside = (source < rows) & (jnp.abs(source - target) <= RIM)
    across = (beyond >= first) & (beyond < first + RIM) & (jnp.abs(place - target) <= RIM)
    band[...] = jnp.where(inside | across, 1.0, 0.0).astype(BF16)
    part[...] = jnp.zeros(part.shape, F32)

    for copy in near:
        copy.wait()

    @pl.loop(0, leads)
    def _(l):
        for g in range(rim.shape[1]):
            tile = rim_in[l, g].astype(F32)
            for s in range(min(per_tile, cols - g * per_tile)):
                lhs[l, g * per_tile + s + RIM, :, rows:] = pltpu.roll(tile, (-SLOT * s) % rows, 1).astype(BF16)

    for side in range(2):
        tile = corner_in[side].astype(F32)
        for l in range(leads):
            for c in range(RIM):
                s = l * RIM + c
                x = side * (cols + RIM) + c
                lhs[l, x, :, :rows] = edge_in[side, s]
                lhs[l, x, :, rows:] = pltpu.roll(tile, (-SLOT * s) % rows, 1).astype(BF16)

    @pl.loop(0, leads)
    def _(l):
        flat = lhs[l].reshape((cols + 2 * RIM) * own_days, 2 * rows)
        product = jnp.dot(flat, band[...], preferred_element_type=F32)
        boxed[l] = product.reshape(cols + 2 * RIM, own_days, rows)

    for copy in masks:
        copy.wait()

    def chunk(q, count):
        start = q * days
        window = []
        for l in range(leads):
            y = [boxed[l, start + i] for i in range(count + 2 * RIM)]
            two = [y[i] + y[i + 1] for i in range(count + 5)]
            window.append([two[i] + two[i + 2] + (two[i + 4] + y[i + 6]) for i in range(count)])
        for l in range(leads):
            masked = [mask_in[g, l, q].astype(F32) for g in range(days)]
            for i in range(count):
                total = window[l][i]
                if l > 0:
                    total = total + window[l - 1][i]
                if l < leads - 1:
                    total = total + window[l + 1][i]
                metric = total * (1.0 / 147.0)
                metric_out[l, start + i] = metric
                weight = (1.0 / (metric + 1e-5)).astype(BF16).astype(F32)
                picked = jnp.zeros((own_days, rows), F32)
                for g in range(days):
                    shift = (share * (g - i)) % rows
                    moved = pltpu.roll(masked[g], shift, 1) if shift else masked[g]
                    picked = jnp.where(part_of == g, moved, picked)
                weight = weight * picked
                part[l, pl.ds(start + i, 1), :] = jnp.sum(
                    weight * obs[l, start + i].astype(F32), axis=0, keepdims=True)
                part[leads + l, pl.ds(start + i, 1), :] = jnp.sum(weight, axis=0, keepdims=True)

    @pl.loop(0, cols // days)
    def _(q):
        chunk(q, days)
    if cols % days:
        chunk(cols // days, cols % days)

    wide = part.shape[1]
    wide_part = lax.broadcasted_iota(jnp.int32, (wide, rows), 1) // share
    partials = []
    for step in [*range(1, days), 0]:
        owner = owners[step]
        for t in range(2):
            total = jnp.ones((wide, rows), F32)
            for l in range(leads):
                shift = lax.rem(share * (l - owner) + rows * days, rows)
                total = jnp.where(wide_part == l, pltpu.roll(part[t * leads + l], shift, 1), total)
            if step:
                part_send[step - 1, t] = total
            else:
                part_in[0, t] = total
        if step:
            partials.append(send(
                part_send.at[step - 1], part_in.at[step], part_ssem.at[step - 1], part_rsem.at[step - 1],
                {"day": owner},
            ))
    flip[...] = jnp.zeros(flip.shape, F32)
    for copy in partials:
        copy.wait()
    numerator, denominator = part_in[0, 0], part_in[0, 1]
    for step in range(1, days):
        numerator = numerator + part_in[step, 0]
        denominator = denominator + part_in[step, 1]
    flip[:wide] = numerator / denominator
    turned = flip[...].T
    for l in range(leads):
        prediction_out[l] = turned[l * share:(l + 1) * share, :cols]


def on_device(days, lons, runs, outlook, scale, obs, chosen):
    runs = jnp.transpose(runs, (1, 2, 3, 0, 4))
    obs = jnp.transpose(obs, (1, 2, 0, 3))
    chosen = jnp.transpose(chosen, (0, 3, 2, 1))
    variables, leads, cols, own_days, rows = runs.shape
    share = rows // days
    groups = -(-cols // days)
    words = days * own_days // 32
    tiles = -(-words * leads // days)
    rims = -(-cols // (rows // SLOT))
    wide = -(-cols // 8) * 8
    tile = (own_days, rows)
    vmem = pl.BlockSpec(memory_space=pltpu.VMEM)
    metric, prediction = pl.pallas_call(
        functools.partial(kernel, days, lons),
        out_shape=(
            jax.ShapeDtypeStruct((leads, cols) + tile, F32),
            jax.ShapeDtypeStruct((leads, share, cols), F32),
        ),
        in_specs=[vmem, vmem, pl.BlockSpec(memory_space=pltpu.SMEM), vmem, vmem],
        out_specs=(vmem, vmem),
        scratch_shapes=[
            pltpu.VMEM((variables * leads, cols, rows), F32),
            pltpu.VMEM((leads, cols + 2 * RIM, own_days, 2 * rows), BF16),
            pltpu.VMEM((2 * rows, rows), BF16),
            pltpu.VMEM((leads, cols + 2 * RIM) + tile, F32),
            pltpu.VMEM((2, leads * RIM) + tile, BF16),
            pltpu.VMEM((2, leads * RIM) + tile, BF16),
            pltpu.VMEM((2,) + tile, BF16),
            pltpu.VMEM((2,) + tile, BF16),
            pltpu.VMEM((leads, rims) + tile, BF16),
            pltpu.VMEM((leads, rims) + tile, BF16),
            pltpu.VMEM((tiles, rows, rows), jnp.int32),
            pltpu.VMEM((tiles, rows, rows), jnp.int32),
            pltpu.VMEM((words * leads, -(-groups // 8) * 8, rows), jnp.int32),
            pltpu.VMEM((days - 1, leads, groups) + tile, BF16),
            pltpu.VMEM((days, leads, groups) + tile, BF16),
            pltpu.VMEM((2 * leads, wide, rows), F32),
            pltpu.VMEM((days - 1, 2, wide, rows), F32),
            pltpu.VMEM((days, 2, wide, rows), F32),
            pltpu.VMEM((rows, rows), F32),
            pltpu.SemaphoreType.DMA((5,)),
            pltpu.SemaphoreType.DMA((5,)),
            pltpu.SemaphoreType.DMA((days - 1,)),
            pltpu.SemaphoreType.DMA((days - 1,)),
            pltpu.SemaphoreType.DMA((days - 1,)),
            pltpu.SemaphoreType.DMA((days - 1,)),
        ],
        compiler_params=pltpu.CompilerParams(
            collective_id=0, has_side_effects=True, vmem_limit_bytes=48 * 2**20
        ),
    )(runs, outlook, scale, obs, chosen)
    return jnp.transpose(metric, (2, 0, 1, 3)), jnp.transpose(prediction, (0, 2, 1))


def solution(mesh):
    in_specs = (
        P("day", None, None, "lon", "lat"),
        P(None, None, "lon", "lat"),
        P(),
        P("day", None, "lon", "lat"),
        P(None, "lon", ("lat", "day"), None),
    )
    out_specs = (P("day", None, "lon", "lat"), P(None, "lon", ("lat", "day")))
    return jax.shard_map(
        functools.partial(on_device, mesh.shape["day"], mesh.shape["lon"]),
        mesh=mesh, in_specs=in_specs, out_specs=out_specs, check_vma=False,
    )
```

time: 147 us -> 29.7 us (0.20); the launches traced: 145 us -> 29.4 us
  local copies, waits for them, and re-layouts: 74.3 us -> 7.21 us
  other arithmetic: 39.2 us -> 0 us
  Pallas kernels: 0 us -> 21.5 us
  starting transfers between devices: 16.7 us -> 0 us
  waiting for transfers between devices: 11.3 us -> 0 us
  matrix products: 2.55 us -> 0 us
    reduce_sum x2 -> x0, other arithmetic: 27.2 us -> none  [the longest x1 24.6 us: on_device(): denominator = jnp.sum(weight_f, axis=0)]
    pallas_call x0 -> x1, Pallas kernels: none -> 21.5 us  [on_device(): pl.pallas_call(functools.partial(kernel, days, lons), out_shape=(jax.Shap...]
    unnamed x36 -> x12, local copies, waits for them, and re-layouts: 26.9 us -> 7.21 us
    eq x22 -> x0, local copies, waits for them, and re-layouts: 14.7 us -> none  [selection(): chosen[None, :, :, :, slot] == days_col]
    slice x3 -> x0, local copies, waits for them, and re-layouts: 13.4 us -> none  [the longest x2 8.96 us: extended(): lax.slice_in_dim(block, block.shape[dim] - width, None, axis=dim)]
    ppermute x4 -> x0, waiting for transfers between devices: 11.3 us -> none  [the longest x2 7.09 us: extended(): lax.ppermute(lax.slice_in_dim(block, block.shape[dim] - width, None, axis...]
    concatenate x2 -> x0, other arithmetic: 9.97 us -> none  [extended(): block = jnp.concatenate([low, block, high], axis=dim)]
    ppermute x2 -> x0, local copies, waits for them, and re-layouts: 8.82 us -> none  [the longest x1 4.48 us: extended(): lax.ppermute(lax.slice_in_dim(block, 0, width, axis=dim), axis, backward)]
  transfers between devices with their start and end apart: 6 -> 0, of which waited for: 2 -> 0; matrix products, arithmetic and copies ran while one was open for 45% -> 0% of each run, Pallas kernels for 0% -> 0%
where the time goes in v1:
time: 29.7 us; the launch traced here: 29.4 us
  Pallas kernels  21.5 us (72%)
  local copies, waits for them, and re-layouts  7.21 us (24%)
  between operations  0.65 us (2%)
    pallas_call x1, Pallas kernels, on_device(): pl.pallas_call(functools.partial(kernel, days, lons), out_shape=(jax.Shap...  21.5 us
    unnamed x12, local copies, waits for them, and re-layouts  7.21 us

profile of v1, /device:TPU:0, one launch (start us, length us, event | category | flops | bytes accessed | tf_op | source)
XLA Modules:
  0.0 29.4 jit_solution(13322701569185735044)
XLA Ops:
  0.6 0.0 copy-start
  0.6 1.8 %copy-done = bf16[16,5,3,45,128]{4,0,3,2,1:T(8,128)(2,1)S(1)} copy-done((bf16[16,5,3,45,128]{4,0,3,2,1:T(8,128)(2,1)S(1)}, bf16[16,5,3,45,128]{4,0,3,2,1:T(8,128)(2,1)}, u32[]{:S(2)}) %copy-start) | copy-done | bytes 2764824
  2.4 0.0 copy-start.1
  2.4 1.2 %copy-done.1 = s32[3,45,32,20]{1,2,3,0:T(8,128)S(1)} copy-done((s32[3,45,32,20]{1,2,3,0:T(8,128)S(1)}, s32[3,45,32,20]{1,2,3,0:T(8,128)}, u32[]{:S(2)}) %copy-start.1) | copy-done | bytes 345624
  3.6 0.0 copy-start.2
  3.6 1.0 %copy-done.2 = bf16[16,3,45,128]{3,0,2,1:T(8,128)(2,1)S(1)} copy-done((bf16[16,3,45,128]{3,0,2,1:T(8,128)(2,1)S(1)}, bf16[16,3,45,128]{3,0,2,1:T(8,128)(2,1)}, u32[]{:S(2)}) %copy-start.2) | copy-done | bytes 552984
  4.7 0.0 copy-start.3
  4.7 0.9 %copy-done.3 = bf16[5,3,45,128]{3,2,1,0:T(8,128)(2,1)S(1)} copy-done((bf16[5,3,45,128]{3,2,1,0:T(8,128)(2,1)S(1)}, bf16[5,3,45,128]{3,2,1,0:T(8,128)(2,1)}, u32[]{:S(2)}) %copy-start.3) | copy-done | bytes 172824
  5.6 0.0 copy-start.4
  5.6 0.7 %copy-done.4 = f32[5]{0:T(128)S(1)} copy-done((f32[5]{0:T(128)S(1)}, f32[5]{0:T(128)}, u32[]{:S(2)}) %copy-start.4) | copy-done | bytes 44
  6.2 21.5 %shard_map.68 = (f32[3,45,16,128]{3,2,1,0:T(8,128)S(1)}, f32[3,32,45]{2,1,0:T(8,128)S(1)}) custom-call(bf16[5,3,45,16,128]{4,3,2,1,0:T(8,128)(2,1)S(1)} %bitcast.5, bf16[5,3,45,128]{3,2,1,0:T(8,128)(2,1)S(1)} %copy-done.3, f32[5]{0:T(128)S(1)} %copy-done.4, bf16[3,45,16,128]{3,2,1,0:T(8,128)(2,1)S(1)} %bitcast.8, s32[3,20,32,45]{3,2,1,0:T(8,128)S(1)} %bitcast.7), custom_call_target="tpu_custom_call" | custom-call | tf_op jit(solution)/shard_map/pallas_call | solution.py:273
  27.8 1.0 %copy.9 = f32[16,3,45,128]{3,0,2,1:T(8,128)} copy(f32[16,3,45,128]{3,0,2,1:T(8,128)S(1)} %bitcast.6) | data formatting | bytes 2211840
  28.8 0.6 %copy.10 = f32[3,45,32]{1,2,0:T(8,128)} copy(f32[3,45,32]{1,2,0:T(8,128)S(1)} %bitcast.9) | data formatting | bytes 34560
Async XLA Ops:
  0.6 1.8 %copy-start = (bf16[16,5,3,45,128]{4,0,3,2,1:T(8,128)(2,1)S(1)}, bf16[16,5,3,45,128]{4,0,3,2,1:T(8,128)(2,1)}, u32[]{:S(2)}) copy-start(bf16[16,5,3,45,128]{4,0,3,2,1:T(8,128)(2,1)} %param.5) | copy-start | bytes 8294404
  2.4 1.2 %copy-start.1 = (s32[3,45,32,20]{1,2,3,0:T(8,128)S(1)}, s32[3,45,32,20]{1,2,3,0:T(8,128)}, u32[]{:S(2)}) copy-start(s32[3,45,32,20]{1,2,3,0:T(8,128)} %param.9) | copy-start | bytes 1036804
  3.6 1.1 %copy-start.2 = (bf16[16,3,45,128]{3,0,2,1:T(8,128)(2,1)S(1)}, bf16[16,3,45,128]{3,0,2,1:T(8,128)(2,1)}, u32[]{:S(2)}) copy-start(bf16[16,3,45,128]{3,0,2,1:T(8,128)(2,1)} %param.8) | copy-start | bytes 1658884
  4.7 0.9 %copy-start.3 = (bf16[5,3,45,128]{3,2,1,0:T(8,128)(2,1)S(1)}, bf16[5,3,45,128]{3,2,1,0:T(8,128)(2,1)}, u32[]{:S(2)}) copy-start(bf16[5,3,45,128]{3,2,1,0:T(8,128)(2,1)} %outlook.1) | copy-start | bytes 518404
  5.6 0.7 %copy-start.4 = (f32[5]{0:T(128)S(1)}, f32[5]{0:T(128)}, u32[]{:S(2)}) copy-start(f32[5]{0:T(128)} %scale.1) | copy-start | bytes 64

commit v2 on v1

--- a/solution.py
+++ b/solution.py
@@ -14,7 +14,8 @@
 
 
 def kernel(
-    days, lons, runs, outlook, scale, obs, chosen, metric_out, prediction_out,
+    days, lons, runs_hbm, outlook_hbm, scale, obs_hbm, chosen_hbm, metric_out, prediction_out,
+    runs, outlook, obs, chosen, load_sem,
     outlook_f, lhs, band, boxed, edge, edge_in, corner, corner_in, rim, rim_in,
     bits, bits_t, packed, mask_send, mask_in, part, part_send, part_in, flip,
     near_send, near_recv, mask_ssem, mask_rsem, part_ssem, part_rsem,
@@ -34,6 +35,18 @@
         {"lat": other},
     ]
     owners = [lax.rem(day + step, days) for step in range(days)]
+    loads = [
+        pltpu.make_async_copy(outlook_hbm, outlook, load_sem.at[0]),
+        pltpu.make_async_copy(runs_hbm.at[:, :, :RIM], runs.at[:, :, :RIM], load_sem.at[1]),
+        pltpu.make_async_copy(runs_hbm.at[:, :, cols - RIM:], runs.at[:, :, cols - RIM:], load_sem.at[2]),
+        pltpu.make_async_copy(chosen_hbm, chosen, load_sem.at[3]),
+        pltpu.make_async_copy(
+            runs_hbm.at[:, :, RIM:cols - RIM], runs.at[:, :, RIM:cols - RIM], load_sem.at[4]),
+        pltpu.make_async_copy(obs_hbm, obs, load_sem.at[5]),
+    ]
+    for load in loads:
+        load.start()
+
     barrier = pltpu.get_barrier_semaphore()
     for device in nearby + [{"day": owner} for owner in owners[1:]]:
         pl.semaphore_signal(barrier, inc=1, device_id=device, device_id_type=pl.DeviceIdType.MESH)
@@ -50,6 +63,7 @@
         copy.start()
         return copy
 
+    loads[0].wait()
     for p in range(variables):
         for l in range(leads):
             outlook_f[p * leads + l] = outlook[p, l].astype(F32)
@@ -68,6 +82,8 @@
             edge[side, l * RIM + x] = value
 
     for side in range(2):
+        loads[1 + side].wait()
+
         @pl.loop(0, RIM)
         def _(x):
             edge_columns(x, side)
@@ -83,6 +99,7 @@
         near.append(send(edge.at[side], edge_in.at[1 - side], near_send.at[side], near_recv.at[side], device))
         near.append(send(corner.at[side], corner_in.at[1 - side], near_send.at[2 + side], near_recv.at[2 + side], across))
 
+    loads[3].wait()
     words = days * own_days // 32
     targets_per_word = 32 // own_days
     for t in range(bits.shape[0]):
@@ -133,6 +150,8 @@
             {"day": owners[step]},
         ))
 
+    loads[4].wait()
+
     @pl.loop(RIM, cols - RIM)
     def _(x):
         for l in range(leads):
@@ -188,6 +207,7 @@
         product = jnp.dot(flat, band[...], preferred_element_type=F32)
         boxed[l] = product.reshape(cols + 2 * RIM, own_days, rows)
 
+    loads[5].wait()
     for copy in masks:
         copy.wait()
 
@@ -270,15 +290,21 @@
     wide = -(-cols // 8) * 8
     tile = (own_days, rows)
     vmem = pl.BlockSpec(memory_space=pltpu.VMEM)
+    hbm = pl.BlockSpec(memory_space=pltpu.HBM)
     metric, prediction = pl.pallas_call(
         functools.partial(kernel, days, lons),
         out_shape=(
             jax.ShapeDtypeStruct((leads, cols) + tile, F32),
             jax.ShapeDtypeStruct((leads, share, cols), F32),
         ),
-        in_specs=[vmem, vmem, pl.BlockSpec(memory_space=pltpu.SMEM), vmem, vmem],
+        in_specs=[hbm, hbm, pl.BlockSpec(memory_space=pltpu.SMEM), hbm, hbm],
         out_specs=(vmem, vmem),
         scratch_shapes=[
+            pltpu.VMEM(runs.shape, BF16),
+            pltpu.VMEM(outlook.shape, BF16),
+            pltpu.VMEM(obs.shape, BF16),
+            pltpu.VMEM(chosen.shape, jnp.int32),
+            pltpu.SemaphoreType.DMA((6,)),
             pltpu.VMEM((variables * leads, cols, rows), F32),
             pltpu.VMEM((leads, cols + 2 * RIM, own_days, 2 * rows), BF16),
             pltpu.VMEM((2 * rows, rows), BF16),

time: 29.7 us -> 30.5 us (1.027)
  Pallas kernels: 21.5 us -> 22.3 us
    pallas_call x1, Pallas kernels: 21.5 us -> 22.3 us  [on_device(): pl.pallas_call(functools.partial(kernel, days, lons), out_shape=(jax.Shap...]
where the time goes in v2:
time: 30.5 us; the launch traced here: 30.2 us
  Pallas kernels  22.3 us (73%)
  local copies, waits for them, and re-layouts  7.21 us (24%)
  between operations  0.65 us (2%)
    pallas_call x1, Pallas kernels, on_device(): pl.pallas_call(functools.partial(kernel, days, lons), out_shape=(jax.Shap...  22.3 us
    unnamed x12, local copies, waits for them, and re-layouts  7.21 us

profile of v2, /device:TPU:0, one launch (start us, length us, event | category | flops | bytes accessed | tf_op | source)
XLA Modules:
  0.0 30.2 jit_solution(11740295970493108993)
XLA Ops:
  0.6 0.0 copy-start
  0.6 1.8 %copy-done = bf16[16,5,3,45,128]{4,0,3,2,1:T(8,128)(2,1)S(1)} copy-done((bf16[16,5,3,45,128]{4,0,3,2,1:T(8,128)(2,1)S(1)}, bf16[16,5,3,45,128]{4,0,3,2,1:T(8,128)(2,1)}, u32[]{:S(2)}) %copy-start) | copy-done | bytes 2764824
  2.4 0.0 copy-start.1
  2.4 1.2 %copy-done.1 = s32[3,45,32,20]{1,2,3,0:T(8,128)S(1)} copy-done((s32[3,45,32,20]{1,2,3,0:T(8,128)S(1)}, s32[3,45,32,20]{1,2,3,0:T(8,128)}, u32[]{:S(2)}) %copy-start.1) | copy-done | bytes 345624
  3.6 0.0 copy-start.2
  3.6 1.0 %copy-done.2 = bf16[16,3,45,128]{3,0,2,1:T(8,128)(2,1)S(1)} copy-done((bf16[16,3,45,128]{3,0,2,1:T(8,128)(2,1)S(1)}, bf16[16,3,45,128]{3,0,2,1:T(8,128)(2,1)}, u32[]{:S(2)}) %copy-start.2) | copy-done | bytes 552984
  4.7 0.0 copy-start.3
  4.7 0.9 %copy-done.3 = bf16[5,3,45,128]{3,2,1,0:T(8,128)(2,1)S(1)} copy-done((bf16[5,3,45,128]{3,2,1,0:T(8,128)(2,1)S(1)}, bf16[5,3,45,128]{3,2,1,0:T(8,128)(2,1)}, u32[]{:S(2)}) %copy-start.3) | copy-done | bytes 172824
  5.6 0.0 copy-start.4
  5.6 0.7 %copy-done.4 = f32[5]{0:T(128)S(1)} copy-done((f32[5]{0:T(128)S(1)}, f32[5]{0:T(128)}, u32[]{:S(2)}) %copy-start.4) | copy-done | bytes 44
  6.2 22.3 %shard_map.68 = (f32[3,45,16,128]{3,2,1,0:T(8,128)S(1)}, f32[3,32,45]{2,1,0:T(8,128)S(1)}) custom-call(bf16[5,3,45,16,128]{4,3,2,1,0:T(8,128)(2,1)S(1)} %bitcast.5, bf16[5,3,45,128]{3,2,1,0:T(8,128)(2,1)S(1)} %copy-done.3, f32[5]{0:T(128)S(1)} %copy-done.4, bf16[3,45,16,128]{3,2,1,0:T(8,128)(2,1)S(1)} %bitcast.8, s32[3,20,32,45]{3,2,1,0:T(8,128)S(1)} %bitcast.7), custom_call_target="tpu_custom_call" | custom-call | tf_op jit(solution)/shard_map/pallas_call | solution.py:294
  28.6 1.0 %copy.9 = f32[16,3,45,128]{3,0,2,1:T(8,128)} copy(f32[16,3,45,128]{3,0,2,1:T(8,128)S(1)} %bitcast.6) | data formatting | bytes 2211840
  29.6 0.6 %copy.10 = f32[3,45,32]{1,2,0:T(8,128)} copy(f32[3,45,32]{1,2,0:T(8,128)S(1)} %bitcast.9) | data formatting | bytes 34560
Async XLA Ops:
  0.6 1.8 %copy-start = (bf16[16,5,3,45,128]{4,0,3,2,1:T(8,128)(2,1)S(1)}, bf16[16,5,3,45,128]{4,0,3,2,1:T(8,128)(2,1)}, u32[]{:S(2)}) copy-start(bf16[16,5,3,45,128]{4,0,3,2,1:T(8,128)(2,1)} %param.5) | copy-start | bytes 8294404
  2.4 1.2 %copy-start.1 = (s32[3,45,32,20]{1,2,3,0:T(8,128)S(1)}, s32[3,45,32,20]{1,2,3,0:T(8,128)}, u32[]{:S(2)}) copy-start(s32[3,45,32,20]{1,2,3,0:T(8,128)} %param.9) | copy-start | bytes 1036804
  3.6 1.1 %copy-start.2 = (bf16[16,3,45,128]{3,0,2,1:T(8,128)(2,1)S(1)}, bf16[16,3,45,128]{3,0,2,1:T(8,128)(2,1)}, u32[]{:S(2)}) copy-start(bf16[16,3,45,128]{3,0,2,1:T(8,128)(2,1)} %param.8) | copy-start | bytes 1658884
  4.7 0.9 %copy-start.3 = (bf16[5,3,45,128]{3,2,1,0:T(8,128)(2,1)S(1)}, bf16[5,3,45,128]{3,2,1,0:T(8,128)(2,1)}, u32[]{:S(2)}) copy-start(bf16[5,3,45,128]{3,2,1,0:T(8,128)(2,1)} %outlook_hbm.1) | copy-start | bytes 518404
  5.6 0.7 %copy-start.4 = (f32[5]{0:T(128)S(1)}, f32[5]{0:T(128)}, u32[]{:S(2)}) copy-start(f32[5]{0:T(128)} %scale.1) | copy-start | bytes 64

commit v3 on v2

--- a/solution.py
+++ b/solution.py
@@ -15,7 +15,7 @@
 
 def kernel(
     days, lons, runs_hbm, outlook_hbm, scale, obs_hbm, chosen_hbm, metric_out, prediction_out,
-    runs, outlook, obs, chosen, load_sem,
+    runs, outlook, obs, chosen, metric_v, weights, load_sem,
     outlook_f, lhs, band, boxed, edge, edge_in, corner, corner_in, rim, rim_in,
     bits, bits_t, packed, mask_send, mask_in, part, part_send, part_in, flip,
     near_send, near_recv, mask_ssem, mask_rsem, part_ssem, part_rsem,
@@ -36,10 +36,10 @@
     ]
     owners = [lax.rem(day + step, days) for step in range(days)]
     loads = [
+        pltpu.make_async_copy(chosen_hbm, chosen, load_sem.at[3]),
         pltpu.make_async_copy(outlook_hbm, outlook, load_sem.at[0]),
         pltpu.make_async_copy(runs_hbm.at[:, :, :RIM], runs.at[:, :, :RIM], load_sem.at[1]),
         pltpu.make_async_copy(runs_hbm.at[:, :, cols - RIM:], runs.at[:, :, cols - RIM:], load_sem.at[2]),
-        pltpu.make_async_copy(chosen_hbm, chosen, load_sem.at[3]),
         pltpu.make_async_copy(
             runs_hbm.at[:, :, RIM:cols - RIM], runs.at[:, :, RIM:cols - RIM], load_sem.at[4]),
         pltpu.make_async_copy(obs_hbm, obs, load_sem.at[5]),
@@ -64,42 +64,6 @@
         return copy
 
     loads[0].wait()
-    for p in range(variables):
-        for l in range(leads):
-            outlook_f[p * leads + l] = outlook[p, l].astype(F32)
-
-    def squares(l, x):
-        total = jnp.zeros((own_days, rows), F32)
-        for p in range(variables):
-            diff = runs[p, l, x].astype(F32) - outlook_f[p * leads + l, pl.ds(x, 1), :]
-            total = total + scale[p] * (diff * diff)
-        return total.astype(BF16)
-
-    def edge_columns(x, side):
-        for l in range(leads):
-            value = squares(l, x + side * (cols - RIM))
-            lhs[l, x + side * (cols - RIM) + RIM, :, :rows] = value
-            edge[side, l * RIM + x] = value
-
-    for side in range(2):
-        loads[1 + side].wait()
-
-        @pl.loop(0, RIM)
-        def _(x):
-            edge_columns(x, side)
-        total = jnp.zeros((own_days, rows), F32)
-        for s in range(leads * RIM):
-            moved = pltpu.roll(edge[side, s].astype(F32), RIM + SLOT * s, 1)
-            total = jnp.where(slot_of == s, moved, total)
-        corner[side] = total.astype(BF16)
-
-    pl.semaphore_wait(barrier, len(nearby) + days - 1)
-    near = []
-    for side, (device, across) in enumerate([(nearby[0], nearby[2]), (nearby[1], nearby[3])]):
-        near.append(send(edge.at[side], edge_in.at[1 - side], near_send.at[side], near_recv.at[side], device))
-        near.append(send(corner.at[side], corner_in.at[1 - side], near_send.at[2 + side], near_recv.at[2 + side], across))
-
-    loads[3].wait()
     words = days * own_days // 32
     targets_per_word = 32 // own_days
     for t in range(bits.shape[0]):
@@ -131,24 +95,66 @@
 
     day_row = lax.broadcasted_iota(jnp.int32, (own_days, rows), 0)
 
-    def expand(owner, store):
+    def expand(owner, l, store):
         shift = day_row + lax.rem(owner, targets_per_word) * own_days
         base = (owner // targets_per_word) * leads
-        for l in range(leads):
-            @pl.loop(0, groups)
-            def _(q):
-                row = jnp.broadcast_to(packed[base + l, pl.ds(q, 1), :], (own_days, rows))
-                store(l, q, (lax.shift_right_logical(row, shift) & 1).astype(F32).astype(BF16))
-
-    masks = []
-    for step in range(1, days):
-        def store(l, q, value):
-            mask_send[step - 1, l, q] = value
-        expand(owners[step], store)
-        masks.append(send(
-            mask_send.at[step - 1], mask_in.at[day], mask_ssem.at[step - 1], mask_rsem.at[step - 1],
-            {"day": owners[step]},
-        ))
+
+        @pl.loop(0, groups)
+        def _(q):
+            row = jnp.broadcast_to(packed[base + l, pl.ds(q, 1), :], (own_days, rows))
+            store(q, (lax.shift_right_logical(row, shift) & 1).astype(F32).astype(BF16))
+
+    masks = [[] for _ in range(leads)]
+
+    def send_masks(l):
+        for step in range(1, days):
+            def store(q, value):
+                mask_send[step - 1, l, q] = value
+            expand(owners[step], l, store)
+            masks[l].append(send(
+                mask_send.at[step - 1, l], mask_in.at[day, l],
+                mask_ssem.at[step - 1, l], mask_rsem.at[step - 1, l], {"day": owners[step]},
+            ))
+
+    pl.semaphore_wait(barrier, len(nearby) + days - 1)
+    send_masks(0)
+    loads[1].wait()
+    for p in range(variables):
+        for l in range(leads):
+            outlook_f[p * leads + l] = outlook[p, l].astype(F32)
+
+    def squares(l, x):
+        total = jnp.zeros((own_days, rows), F32)
+        for p in range(variables):
+            diff = runs[p, l, x].astype(F32) - outlook_f[p * leads + l, pl.ds(x, 1), :]
+            total = total + scale[p] * (diff * diff)
+        return total.astype(BF16)
+
+    def edge_columns(x, side):
+        for l in range(leads):
+            value = squares(l, x + side * (cols - RIM))
+            lhs[l, x + side * (cols - RIM) + RIM, :, :rows] = value
+            edge[side, l * RIM + x] = value
+
+    for side in range(2):
+        loads[2 + side].wait()
+
+        @pl.loop(0, RIM)
+        def _(x):
+            edge_columns(x, side)
+        total = jnp.zeros((own_days, rows), F32)
+        for s in range(leads * RIM):
+            moved = pltpu.roll(edge[side, s].astype(F32), RIM + SLOT * s, 1)
+            total = jnp.where(slot_of == s, moved, total)
+        corner[side] = total.astype(BF16)
+
+    near = []
+    for side, (device, across) in enumerate([(nearby[0], nearby[2]), (nearby[1], nearby[3])]):
+        near.append(send(edge.at[side], edge_in.at[1 - side], near_send.at[side], near_recv.at[side], device))
+        near.append(send(corner.at[side], corner_in.at[1 - side], near_send.at[2 + side], near_recv.at[2 + side], across))
+
+    for l in range(1, leads):
+        send_masks(l)
 
     loads[4].wait()
 
@@ -168,9 +174,10 @@
 
     near.append(send(rim, rim_in, near_send.at[4], near_recv.at[4], nearby[4]))
 
-    def own_store(l, q, value):
-        mask_in[day, l, q] = value
-    expand(owners[0], own_store)
+    for l in range(leads):
+        def own_store(q, value):
+            mask_in[day, l, q] = value
+        expand(owners[0], l, own_store)
 
     source = lax.broadcasted_iota(jnp.int32, (2 * rows, rows), 0)
     target = lax.broadcasted_iota(jnp.int32, (2 * rows, rows), 1)
@@ -207,19 +214,13 @@
         product = jnp.dot(flat, band[...], preferred_element_type=F32)
         boxed[l] = product.reshape(cols + 2 * RIM, own_days, rows)
 
-    loads[5].wait()
-    for copy in masks:
-        copy.wait()
-
-    def chunk(q, count):
-        start = q * days
+    def weigh(start, count):
         window = []
         for l in range(leads):
             y = [boxed[l, start + i] for i in range(count + 2 * RIM)]
             two = [y[i] + y[i + 1] for i in range(count + 5)]
             window.append([two[i] + two[i + 2] + (two[i + 4] + y[i + 6]) for i in range(count)])
         for l in range(leads):
-            masked = [mask_in[g, l, q].astype(F32) for g in range(days)]
             for i in range(count):
                 total = window[l][i]
                 if l > 0:
@@ -227,51 +228,76 @@
                 if l < leads - 1:
                     total = total + window[l + 1][i]
                 metric = total * (1.0 / 147.0)
-                metric_out[l, start + i] = metric
-                weight = (1.0 / (metric + 1e-5)).astype(BF16).astype(F32)
-                picked = jnp.zeros((own_days, rows), F32)
-                for g in range(days):
-                    shift = (share * (g - i)) % rows
-                    moved = pltpu.roll(masked[g], shift, 1) if shift else masked[g]
-                    picked = jnp.where(part_of == g, moved, picked)
-                weight = weight * picked
-                part[l, pl.ds(start + i, 1), :] = jnp.sum(
-                    weight * obs[l, start + i].astype(F32), axis=0, keepdims=True)
-                part[leads + l, pl.ds(start + i, 1), :] = jnp.sum(weight, axis=0, keepdims=True)
+                metric_v[l, start + i] = metric
+                weights[l, start + i] = (1.0 / (metric + 1e-5)).astype(BF16)
 
     @pl.loop(0, cols // days)
     def _(q):
-        chunk(q, days)
+        weigh(q * days, days)
     if cols % days:
-        chunk(cols // days, cols % days)
-
-    wide = part.shape[1]
-    wide_part = lax.broadcasted_iota(jnp.int32, (wide, rows), 1) // share
+        weigh(cols - cols % days, cols % days)
+    metric_copy = pltpu.make_async_copy(metric_v, metric_out, load_sem.at[6])
+    metric_copy.start()
+
+    loads[5].wait()
+
+    def pick(l, q, count):
+        masked = [mask_in[g, l, q].astype(F32) for g in range(days)]
+        for i in range(count):
+            x = q * days + i
+            picked = jnp.zeros((own_days, rows), F32)
+            for g in range(days):
+                shift = (share * (g - i)) % rows
+                moved = pltpu.roll(masked[g], shift, 1) if shift else masked[g]
+                picked = jnp.where(part_of == g, moved, picked)
+            weight = weights[l, x].astype(F32) * picked
+            part[0, pl.ds(x, 1), :] = jnp.sum(weight * obs[l, x].astype(F32), axis=0, keepdims=True)
+            part[1, pl.ds(x, 1), :] = jnp.sum(weight, axis=0, keepdims=True)
+
+    half = part.shape[1] // 2
+    half_part = lax.broadcasted_iota(jnp.int32, (half, rows), 1) // share
     partials = []
-    for step in [*range(1, days), 0]:
-        owner = owners[step]
-        for t in range(2):
-            total = jnp.ones((wide, rows), F32)
-            for l in range(leads):
-                shift = lax.rem(share * (l - owner) + rows * days, rows)
-                total = jnp.where(wide_part == l, pltpu.roll(part[t * leads + l], shift, 1), total)
+    for l in range(leads):
+        for copy in masks[l]:
+            copy.wait()
+
+        @pl.loop(0, cols // days)
+        def _(q):
+            pick(l, q, days)
+        if cols % days:
+            pick(l, cols // days, cols % days)
+
+        for step in [*range(1, days), 0]:
+            total = jnp.zeros((half, rows), F32)
+            for slot in range(4):
+                shift = lax.rem(share * (slot - owners[step]) + rows * days, rows)
+                at = half * (slot // 2)
+                moved = pltpu.roll(part[slot % 2, at:at + half, :], shift, 1)
+                total = jnp.where(half_part == slot, moved, total)
             if step:
-                part_send[step - 1, t] = total
+                part_send[step - 1, l] = total
+                partials.append(send(
+                    part_send.at[step - 1, l], part_in.at[step, l],
+                    part_ssem.at[step - 1, l], part_rsem.at[step - 1, l], {"day": owners[step]},
+                ))
             else:
-                part_in[0, t] = total
-        if step:
-            partials.append(send(
-                part_send.at[step - 1], part_in.at[step], part_ssem.at[step - 1], part_rsem.at[step - 1],
-                {"day": owner},
-            ))
+                part_in[0, l] = total
     flip[...] = jnp.zeros(flip.shape, F32)
+    metric_copy.wait()
     for copy in partials:
         copy.wait()
-    numerator, denominator = part_in[0, 0], part_in[0, 1]
-    for step in range(1, days):
-        numerator = numerator + part_in[step, 0]
-        denominator = denominator + part_in[step, 1]
-    flip[:wide] = numerator / denominator
+    halves = [jnp.zeros((half, rows), F32) for _ in range(2)]
+    for l in range(leads):
+        total = part_in[0, l]
+        for step in range(1, days):
+            total = total + part_in[step, l]
+        ratio = total / pltpu.roll(total, rows - share, 1)
+        for h in range(2):
+            shift = (share * (l - 2 * h)) % rows
+            moved = pltpu.roll(ratio, shift, 1) if shift else ratio
+            halves[h] = jnp.where(half_part == l, moved, halves[h])
+    for h in range(2):
+        flip[half * h:half * (h + 1)] = halves[h]
     turned = flip[...].T
     for l in range(leads):
         prediction_out[l] = turned[l * share:(l + 1) * share, :cols]
@@ -287,7 +313,7 @@
     words = days * own_days // 32
     tiles = -(-words * leads // days)
     rims = -(-cols // (rows // SLOT))
-    wide = -(-cols // 8) * 8
+    wide = -(-cols // 16) * 16
     tile = (own_days, rows)
     vmem = pl.BlockSpec(memory_space=pltpu.VMEM)
     hbm = pl.BlockSpec(memory_space=pltpu.HBM)
@@ -298,13 +324,15 @@
             jax.ShapeDtypeStruct((leads, share, cols), F32),
         ),
         in_specs=[hbm, hbm, pl.BlockSpec(memory_space=pltpu.SMEM), hbm, hbm],
-        out_specs=(vmem, vmem),
+        out_specs=(hbm, vmem),
         scratch_shapes=[
             pltpu.VMEM(runs.shape, BF16),
             pltpu.VMEM(outlook.shape, BF16),
             pltpu.VMEM(obs.shape, BF16),
             pltpu.VMEM(chosen.shape, jnp.int32),
-            pltpu.SemaphoreType.DMA((6,)),
+            pltpu.VMEM((leads, cols) + tile, F32),
+            pltpu.VMEM((leads, cols) + tile, BF16),
+            pltpu.SemaphoreType.DMA((7,)),
             pltpu.VMEM((variables * leads, cols, rows), F32),
             pltpu.VMEM((leads, cols + 2 * RIM, own_days, 2 * rows), BF16),
             pltpu.VMEM((2 * rows, rows), BF16),
@@ -320,19 +348,19 @@
             pltpu.VMEM((words * leads, -(-groups // 8) * 8, rows), jnp.int32),
             pltpu.VMEM((days - 1, leads, groups) + tile, BF16),
             pltpu.VMEM((days, leads, groups) + tile, BF16),
-            pltpu.VMEM((2 * leads, wide, rows), F32),
-            pltpu.VMEM((days - 1, 2, wide, rows), F32),
-            pltpu.VMEM((days, 2, wide, rows), F32),
+            pltpu.VMEM((2, wide, rows), F32),
+            pltpu.VMEM((days - 1, leads, wide // 2, rows), F32),
+            pltpu.VMEM((days, leads, wide // 2, rows), F32),
             pltpu.VMEM((rows, rows), F32),
             pltpu.SemaphoreType.DMA((5,)),
             pltpu.SemaphoreType.DMA((5,)),
-            pltpu.SemaphoreType.DMA((days - 1,)),
-            pltpu.SemaphoreType.DMA((days - 1,)),
-            pltpu.SemaphoreType.DMA((days - 1,)),
-            pltpu.SemaphoreType.DMA((days - 1,)),
+            pltpu.SemaphoreType.DMA((days - 1, leads)),
+            pltpu.SemaphoreType.DMA((days - 1, leads)),
+            pltpu.SemaphoreType.DMA((days - 1, leads)),
+            pltpu.SemaphoreType.DMA((days - 1, leads)),
         ],
         compiler_params=pltpu.CompilerParams(
-            collective_id=0, has_side_effects=True, vmem_limit_bytes=48 * 2**20
+            collective_id=0, has_side_effects=True, vmem_limit_bytes=64 * 2**20 - 2**16
         ),
     )(runs, outlook, scale, obs, chosen)
     return jnp.transpose(metric, (2, 0, 1, 3)), jnp.transpose(prediction, (0, 2, 1))

time: 30.5 us -> 25.6 us (0.84)
  local copies, waits for them, and re-layouts: 7.21 us -> 2.96 us
  Pallas kernels: 22.3 us -> 21.8 us
    unnamed x12 -> x4, local copies, waits for them, and re-layouts: 7.21 us -> 2.96 us
    pallas_call x1, Pallas kernels: 22.3 us -> 21.8 us  [on_device(): pl.pallas_call(functools.partial(kernel, days, lons), out_shape=(jax.Shap...]
where the time goes in v3:
time: 25.6 us; the launch traced here: 25.4 us
  Pallas kernels  21.8 us (85%)
  local copies, waits for them, and re-layouts  2.96 us (12%)
  between operations  0.65 us (3%)
    pallas_call x1, Pallas kernels, on_device(): pl.pallas_call(functools.partial(kernel, days, lons), out_shape=(jax.Shap...  21.8 us
    unnamed x4, local copies, waits for them, and re-layouts  2.96 us

profile of v3, /device:TPU:0, one launch (start us, length us, event | category | flops | bytes accessed | tf_op | source)
XLA Modules:
  0.0 25.4 jit_solution(2190223907572225464)
XLA Ops:
  0.6 21.8 %shard_map.68 = (f32[3,45,16,128]{3,2,1,0:T(8,128)}, f32[3,32,45]{2,1,0:T(8,128)}) custom-call(bf16[5,3,45,16,128]{4,3,2,1,0:T(8,128)(2,1)} %bitcast.5, bf16[5,3,45,128]{3,2,1,0:T(8,128)(2,1)} %outlook_hbm.1, f32[5]{0:T(128)} %scale.1, bf16[3,45,16,128]{3,2,1,0:T(8,128)(2,1)} %bitcast.8, s32[3,20,32,45]{3,2,1,0:T(8,128)} %bitcast.7), custom_call_target="tpu_custom_call" | custom-call | tf_op jit(solution)/shard_map/pallas_call | solution.py:320
  22.5 0.0 copy-start
  22.5 2.3 %copy.9 = f32[16,3,45,128]{3,0,2,1:T(8,128)} copy(f32[16,3,45,128]{3,0,2,1:T(8,128)} %bitcast.6) | data formatting | bytes 2211840
  24.8 0.0 copy-done
  24.8 0.6 %copy.10 = f32[3,45,32]{1,2,0:T(8,128)} copy(f32[3,45,32]{1,2,0:T(8,128)S(1)} %bitcast.9) | data formatting | bytes 34560
Async XLA Ops:
  22.5 2.3 %copy-start = (f32[3,32,45]{2,1,0:T(8,128)S(1)}, f32[3,32,45]{2,1,0:T(8,128)}, u32[]{:S(2)}) copy-start(f32[3,32,45]{2,1,0:T(8,128)} %get-tuple-element.5) | copy-start | bytes 51844

commit v4 on v3

--- a/solution.py
+++ b/solution.py
@@ -16,7 +16,7 @@
 def kernel(
     days, lons, runs_hbm, outlook_hbm, scale, obs_hbm, chosen_hbm, metric_out, prediction_out,
     runs, outlook, obs, chosen, metric_v, weights, load_sem,
-    outlook_f, lhs, band, boxed, edge, edge_in, corner, corner_in, rim, rim_in,
+    outlook_f, local, inner, cross, boxed, edge, edge_in, corner, corner_in, rim, rim_in,
     bits, bits_t, packed, mask_send, mask_in, part, part_send, part_in, flip,
     near_send, near_recv, mask_ssem, mask_rsem, part_ssem, part_rsem,
 ):
@@ -133,7 +133,7 @@
     def edge_columns(x, side):
         for l in range(leads):
             value = squares(l, x + side * (cols - RIM))
-            lhs[l, x + side * (cols - RIM) + RIM, :, :rows] = value
+            local[l, x + side * (cols - RIM)] = value
             edge[side, l * RIM + x] = value
 
     for side in range(2):
@@ -153,7 +153,7 @@
         near.append(send(edge.at[side], edge_in.at[1 - side], near_send.at[side], near_recv.at[side], device))
         near.append(send(corner.at[side], corner_in.at[1 - side], near_send.at[2 + side], near_recv.at[2 + side], across))
 
-    for l in range(1, leads):
+    for l in range(1, leads - 1):
         send_masks(l)
 
     loads[4].wait()
@@ -161,58 +161,70 @@
     @pl.loop(RIM, cols - RIM)
     def _(x):
         for l in range(leads):
-            lhs[l, x + RIM, :, :rows] = squares(l, x)
+            local[l, x] = squares(l, x)
 
     @pl.loop(0, leads)
     def _(l):
         for g in range(rim.shape[1]):
             total = jnp.zeros((own_days, rows), F32)
             for s in range(min(per_tile, cols - g * per_tile)):
-                tile = lhs[l, g * per_tile + s + RIM, :, :rows].astype(F32)
+                tile = local[l, g * per_tile + s].astype(F32)
                 total = jnp.where(slot_of == s, pltpu.roll(tile, (RIM + SLOT * s) % rows, 1), total)
             rim[l, g] = total.astype(BF16)
 
     near.append(send(rim, rim_in, near_send.at[4], near_recv.at[4], nearby[4]))
 
+    send_masks(leads - 1)
     for l in range(leads):
         def own_store(q, value):
             mask_in[day, l, q] = value
         expand(owners[0], l, own_store)
 
-    source = lax.broadcasted_iota(jnp.int32, (2 * rows, rows), 0)
-    target = lax.broadcasted_iota(jnp.int32, (2 * rows, rows), 1)
-    beyond = source - rows
-    place = beyond - RIM + rows * other
+    source = lax.broadcasted_iota(jnp.int32, (rows, rows), 0)
+    target = lax.broadcasted_iota(jnp.int32, (rows, rows), 1)
+    inner[...] = jnp.where(jnp.abs(source - target) <= RIM, 1.0, 0.0).astype(BF16)
+    out_at, in_at = target % SLOT, source % SLOT
+    row_out = jnp.where(out_at < RIM, rows - RIM + out_at, out_at - RIM)
+    row_in = in_at - RIM + rows * other
     first = RIM * other
-    inside = (source < rows) & (jnp.abs(source - target) <= RIM)
-    across = (beyond >= first) & (beyond < first + RIM) & (jnp.abs(place - target) <= RIM)
-    band[...] = jnp.where(inside | across, 1.0, 0.0).astype(BF16)
+    cross[...] = jnp.where(
+        (source // SLOT == target // SLOT) & (out_at < 2 * RIM) & (in_at >= first)
+        & (in_at < first + RIM) & (jnp.abs(row_in - row_out) <= RIM), 1.0, 0.0).astype(BF16)
     part[...] = jnp.zeros(part.shape, F32)
 
-    for copy in near:
+    @pl.loop(0, leads)
+    def _(l):
+        product = jnp.dot(
+            local[l].reshape(cols * own_days, rows), inner[...], preferred_element_type=F32)
+        boxed[l, RIM:RIM + cols] = product.reshape(cols, own_days, rows)
+
+    outer = (lane < RIM) | (lane >= rows - RIM)
+
+    def unpacked(product, s):
+        return jnp.where(outer, pltpu.roll(product, (rows - RIM - SLOT * s) % rows, 1), 0.0)
+
+    for copy in near[:4]:
+        copy.wait()
+    for side in range(2):
+        flat = edge_in[side].reshape(leads * RIM * own_days, rows)
+        sides = jnp.dot(flat, inner[...], preferred_element_type=F32)
+        sides = sides.reshape(leads * RIM, own_days, rows)
+        product = jnp.dot(corner_in[side], cross[...], preferred_element_type=F32)
+        for l in range(leads):
+            for c in range(RIM):
+                s = l * RIM + c
+                boxed[l, side * (cols + RIM) + c] = sides[s] + unpacked(product, s)
+
+    for copy in near[4:]:
         copy.wait()
 
     @pl.loop(0, leads)
     def _(l):
         for g in range(rim.shape[1]):
-            tile = rim_in[l, g].astype(F32)
+            product = jnp.dot(rim_in[l, g], cross[...], preferred_element_type=F32)
             for s in range(min(per_tile, cols - g * per_tile)):
-                lhs[l, g * per_tile + s + RIM, :, rows:] = pltpu.roll(tile, (-SLOT * s) % rows, 1).astype(BF16)
-
-    for side in range(2):
-        tile = corner_in[side].astype(F32)
-        for l in range(leads):
-            for c in range(RIM):
-                s = l * RIM + c
-                x = side * (cols + RIM) + c
-                lhs[l, x, :, :rows] = edge_in[side, s]
-                lhs[l, x, :, rows:] = pltpu.roll(tile, (-SLOT * s) % rows, 1).astype(BF16)
-
-    @pl.loop(0, leads)
-    def _(l):
-        flat = lhs[l].reshape((cols + 2 * RIM) * own_days, 2 * rows)
-        product = jnp.dot(flat, band[...], preferred_element_type=F32)
-        boxed[l] = product.reshape(cols + 2 * RIM, own_days, rows)
+                x = g * per_tile + s + RIM
+                boxed[l, x] = boxed[l, x] + unpacked(product, s)
 
     def weigh(start, count):
         window = []
@@ -301,6 +313,20 @@
     turned = flip[...].T
     for l in range(leads):
         prediction_out[l] = turned[l * share:(l + 1) * share, :cols]
+
+
+def hand_over(metric, prediction, metric_out, prediction_out, sem):
+    leads, cols = metric.shape[:2]
+    copies = [pltpu.make_async_copy(prediction, prediction_out, sem.at[2 * leads])]
+    for l in range(leads):
+        for h in range(2):
+            part = pl.ds(h * (cols // 2), cols // 2 + h * (cols % 2))
+            copies.append(pltpu.make_async_copy(
+                metric.at[l, part], metric_out.at[l, part], sem.at[2 * l + h]))
+    for copy in copies:
+        copy.start()
+    for copy in copies:
+        copy.wait()
 
 
 def on_device(days, lons, runs, outlook, scale, obs, chosen):
@@ -334,8 +360,9 @@
             pltpu.VMEM((leads, cols) + tile, BF16),
             pltpu.SemaphoreType.DMA((7,)),
             pltpu.VMEM((variables * leads, cols, rows), F32),
-            pltpu.VMEM((leads, cols + 2 * RIM, own_days, 2 * rows), BF16),
-            pltpu.VMEM((2 * rows, rows), BF16),
+            pltpu.VMEM((leads, cols) + tile, BF16),
+            pltpu.VMEM((rows, rows), BF16),
+            pltpu.VMEM((rows, rows), BF16),
             pltpu.VMEM((leads, cols + 2 * RIM) + tile, F32),
             pltpu.VMEM((2, leads * RIM) + tile, BF16),
             pltpu.VMEM((2, leads * RIM) + tile, BF16),
@@ -363,6 +390,17 @@
             collective_id=0, has_side_effects=True, vmem_limit_bytes=64 * 2**20 - 2**16
         ),
     )(runs, outlook, scale, obs, chosen)
+    metric, prediction = pl.pallas_call(
+        hand_over,
+        out_shape=(
+            jax.ShapeDtypeStruct(metric.shape, F32),
+            jax.ShapeDtypeStruct(prediction.shape, F32),
+        ),
+        in_specs=[hbm, hbm],
+        out_specs=(hbm, hbm),
+        scratch_shapes=[pltpu.SemaphoreType.DMA((2 * leads + 1,))],
+        compiler_params=pltpu.CompilerParams(vmem_limit_bytes=64 * 2**20 - 2**16),
+    )(metric, prediction)
     return jnp.transpose(metric, (2, 0, 1, 3)), jnp.transpose(prediction, (0, 2, 1))
 
 

time: 25.6 us -> 58.7 us (2.29)
  Pallas kernels: 21.8 us -> 57.9 us
  local copies, waits for them, and re-layouts: 2.96 us -> 0 us
    pallas_call x0 -> x1, Pallas kernels: none -> 36.2 us  [on_device(): pl.pallas_call(hand_over, out_shape=(jax.ShapeDtypeStruct(metric.shape, F...]
    unnamed x4 -> x0, local copies, waits for them, and re-layouts: 2.96 us -> none
where the time goes in v4:
time: 58.7 us; the launch traced here: 58.5 us
  Pallas kernels  57.9 us (99%)
  between operations  0.64 us (1%)
    pallas_call x1, Pallas kernels, on_device(): pl.pallas_call(hand_over, out_shape=(jax.ShapeDtypeStruct(metric.shape, F...  36.2 us
    pallas_call x1, Pallas kernels, on_device(): pl.pallas_call(functools.partial(kernel, days, lons), out_shape=(jax.Shap...  21.7 us

profile of v4, /device:TPU:0, one launch (start us, length us, event | category | flops | bytes accessed | tf_op | source)
XLA Modules:
  0.0 58.5 jit_solution(12500269969584898107)
XLA Ops:
  0.6 21.7 %shard_map.68 = (f32[3,45,16,128]{3,2,1,0:T(8,128)}, f32[3,32,45]{2,1,0:T(8,128)}) custom-call(bf16[5,3,45,16,128]{4,3,2,1,0:T(8,128)(2,1)} %bitcast.5, bf16[5,3,45,128]{3,2,1,0:T(8,128)(2,1)} %outlook_hbm.1, f32[5]{0:T(128)} %scale.1, bf16[3,45,16,128]{3,2,1,0:T(8,128)(2,1)} %bitcast.7, s32[3,20,32,45]{3,2,1,0:T(8,128)} %bitcast.6), custom_call_target="tpu_custom_call" | custom-call | tf_op jit(solution)/shard_map/pallas_call | solution.py:346
  22.4 36.2 %shard_map.69 = (f32[3,45,16,128]{3,2,1,0:T(8,128)}, f32[3,32,45]{2,1,0:T(8,128)}) custom-call(f32[3,45,16,128]{3,2,1,0:T(8,128)} %get-tuple-element.6.metric, f32[3,32,45]{2,1,0:T(8,128)} %get-tuple-element.7.prediction), custom_call_target="tpu_custom_call" | custom-call | tf_op jit(solution)/shard_map/pallas_call | solution.py:393

commit v5 on v4

--- a/solution.py
+++ b/solution.py
@@ -315,18 +315,22 @@
         prediction_out[l] = turned[l * share:(l + 1) * share, :cols]
 
 
-def hand_over(metric, prediction, metric_out, prediction_out, sem):
+def hand_over(metric, prediction, metric_out, prediction_out, metric_v, prediction_v, sem):
     leads, cols = metric.shape[:2]
-    copies = [pltpu.make_async_copy(prediction, prediction_out, sem.at[2 * leads])]
+    pieces = [(prediction, prediction_v, prediction_out)]
     for l in range(leads):
         for h in range(2):
-            part = pl.ds(h * (cols // 2), cols // 2 + h * (cols % 2))
-            copies.append(pltpu.make_async_copy(
-                metric.at[l, part], metric_out.at[l, part], sem.at[2 * l + h]))
-    for copy in copies:
-        copy.start()
-    for copy in copies:
-        copy.wait()
+            at = (l, pl.ds(h * (cols // 2), cols // 2 + h * (cols % 2)))
+            pieces.append((metric.at[at], metric_v.at[at], metric_out.at[at]))
+    loads = [pltpu.make_async_copy(src, mid, sem.at[0, i]) for i, (src, mid, _) in enumerate(pieces)]
+    stores = [pltpu.make_async_copy(mid, dst, sem.at[1, i]) for i, (_, mid, dst) in enumerate(pieces)]
+    for load in loads:
+        load.start()
+    for load, store in zip(loads, stores):
+        load.wait()
+        store.start()
+    for store in stores:
+        store.wait()
 
 
 def on_device(days, lons, runs, outlook, scale, obs, chosen):
@@ -398,7 +402,11 @@
         ),
         in_specs=[hbm, hbm],
         out_specs=(hbm, hbm),
-        scratch_shapes=[pltpu.SemaphoreType.DMA((2 * leads + 1,))],
+        scratch_shapes=[
+            pltpu.VMEM(metric.shape, F32),
+            pltpu.VMEM(prediction.shape, F32),
+            pltpu.SemaphoreType.DMA((2, 2 * leads + 1)),
+        ],
         compiler_params=pltpu.CompilerParams(vmem_limit_bytes=64 * 2**20 - 2**16),
     )(metric, prediction)
     return jnp.transpose(metric, (2, 0, 1, 3)), jnp.transpose(prediction, (0, 2, 1))

time: 58.7 us -> 24.7 us (0.42)
  Pallas kernels: 57.9 us -> 23.9 us
    pallas_call x1, Pallas kernels: 36.2 us -> 2.14 us  [on_device(): pl.pallas_call(hand_over, out_shape=(jax.ShapeDtypeStruct(metric.shape, F...]
where the time goes in v5:
time: 24.7 us; the launch traced here: 24.5 us
  Pallas kernels  23.9 us (97%)
  between operations  0.64 us (3%)
    pallas_call x1, Pallas kernels, on_device(): pl.pallas_call(functools.partial(kernel, days, lons), out_shape=(jax.Shap...  21.7 us
    pallas_call x1, Pallas kernels, on_device(): pl.pallas_call(hand_over, out_shape=(jax.ShapeDtypeStruct(metric.shape, F...  2.14 us

profile of v5, /device:TPU:0, one launch (start us, length us, event | category | flops | bytes accessed | tf_op | source)
XLA Modules:
  0.0 24.5 jit_solution(7691316689822714689)
XLA Ops:
  0.6 21.7 %shard_map.68 = (f32[3,45,16,128]{3,2,1,0:T(8,128)}, f32[3,32,45]{2,1,0:T(8,128)}) custom-call(bf16[5,3,45,16,128]{4,3,2,1,0:T(8,128)(2,1)} %bitcast.5, bf16[5,3,45,128]{3,2,1,0:T(8,128)(2,1)} %outlook_hbm.1, f32[5]{0:T(128)} %scale.1, bf16[3,45,16,128]{3,2,1,0:T(8,128)(2,1)} %bitcast.7, s32[3,20,32,45]{3,2,1,0:T(8,128)} %bitcast.6), custom_call_target="tpu_custom_call" | custom-call | tf_op jit(solution)/shard_map/pallas_call | solution.py:350
  22.4 2.1 %shard_map.69 = (f32[3,45,16,128]{3,2,1,0:T(8,128)}, f32[3,32,45]{2,1,0:T(8,128)}) custom-call(f32[3,45,16,128]{3,2,1,0:T(8,128)} %get-tuple-element.6.metric, f32[3,32,45]{2,1,0:T(8,128)} %get-tuple-element.7.prediction), custom_call_target="tpu_custom_call" | custom-call | tf_op jit(solution)/shard_map/pallas_call | solution.py:397
